TPU v7x, 512 devices: a whole 4x4x16 slice. The times are simulated.
512 devices in a mesh: row: 16 (over x, z_lo), col: 32 (over z_hi, y, core).
Axes of the slice: x: 4, y: 4, z: 16 (z_hi: 4, z_lo: 4; z = z_hi * 4 + z_lo), core: 2. Of those that a mesh axis runs over, the one named last changes fastest.
Arguments:
- iterate: bfloat16 [5120, 24576], P('row', 'col'), may hold values from -0.0234375 to 0.0234375
Outputs:
- update: float32 [5120, 24576], P('row', 'col')
All inputs are finite; a program needn't handle non-finite values.
Results may differ from a plain program's by a relative error of at most 0.0047.
Values may be sent and summed in bfloat16 or wider, within the bound.
A program may use at most 64 MiB of HBM per device.

v0:
```python
import jax
import jax.numpy as jnp
from jax import lax
from jax.sharding import PartitionSpec as P

HID = 24576


def shifted(block, axis, distance):
    devices = range(lax.axis_size(axis))
    route = [((i - distance) % len(devices), i) for i in devices]
    return lax.ppermute(block, axis, route)


def local(iterate):
    rows = iterate.shape[0]
    count = lax.axis_size("row")
    half = count // 2
    mine = lax.axis_index("row")
    gathered = lax.all_gather(iterate, "row", axis=0, tiled=True)
    rolled = jnp.roll(gathered, -mine * rows, axis=0)
    band_rows = rolled[: (half + 1) * rows]
    band = lax.dot_general(
        iterate, band_rows, (((1,), (1,)), ((), ())), preferred_element_type=jnp.float32
    )
    gram = lax.psum(band, "col").astype(jnp.bfloat16)
    pieces = [gram]
    for offset in range(half - 1, 0, -1):
        tile = gram[:, offset * rows : (offset + 1) * rows]
        arrived = shifted(tile, "row", offset)
        pieces.append(arrived.T)
    row_block = jnp.concatenate(pieces, axis=1)
    image = jnp.dot(row_block, rolled, preferred_element_type=jnp.float32).astype(jnp.bfloat16)
    image_all = lax.all_gather(image, "row", axis=0, tiled=True)
    image_rolled = jnp.roll(image_all, -mine * rows, axis=0)
    second = jnp.dot(row_block, image_rolled, preferred_element_type=jnp.float32)
    factor = 0.2 * HID**0.5
    return factor * (
        3.4445 * iterate.astype(jnp.float32) - 4.775 * image.astype(jnp.float32) + 2.0315 * second
    )


def solution(mesh):
    in_specs = (P("row", "col"),)
    out_specs = P("row", "col")
    return jax.shard_map(local, mesh=mesh, in_specs=in_specs, out_specs=out_specs, check_vma=False)
```

profile of v0, /device:TPU:1, one launch (start us, length us, event | category | flops | bytes accessed | tf_op | source)
XLA Modules:
  0.0 729.2 jit_solution(9921533579698452613)
XLA Ops:
  6.5 0.0 all-gather.3.cloned.1.call-start
  6.5 0.7 all-gather.3.cloned.1.call-update
  7.3 0.0 all-gather.5.cloned.1.call-start
  7.3 0.0 copy-start.1
  7.3 187.4 %all-gather.3.cloned.1.call-done = bf16[5120,768]{1,0:T(8,128)(2,1)} async-done(((bf16[320,768]{1,0:T(8,128)(2,1)}), bf16[5120,768]{1,0:T(8,128)(2,1)}) %all-gather.3.cloned.1.call-update) | async-done | bytes 7864336 | tf_op jit(solution)/shard_map/all_gather | solution.py:20
  194.8 13.9 %fusion.1 = bf16[5120,768]{1,0:T(8,128)(2,1)} fusion(s32[]{:T(128)S(6)} %select_n.13, bf16[5120,768]{1,0:T(8,128)(2,1)} %all-gather.3.cloned.1.call-done), kind=kLoop, calls=%fused_computation.5 | loop fusion | flops 15728640 | bytes 15728644 | tf_op jit(solution)/shard_map/jit(_roll_dynamic)/concatenate | solution.py:21
  208.7 0.0 copy-done.1
  208.7 5.9 fusion.6
  214.6 232.5 %all-reduce.1 = bf16[320,2880]{1,0:T(8,128)(2,1)S(1)} all-reduce(f32[320,2880]{1,0:T(8,128)} %fusion.6), channel_id=1, replica_groups=mesh['row'=16,'col'=32] {'col'}, use_global_device_ids=true, to_apply=%region_0.2 | all-reduce | flops 921600 | bytes 5529600 | tf_op jit(solution)/shard_map/psum | solution.py:26
  447.1 1.1 fusion.20
  448.2 1.8 copy.14
  450.0 1.9 collective-permute-start.5
  451.9 0.9 copy.9
  452.8 23.7 %collective-permute-start = (bf16[320,320]{0,1:T(8,128)(2,1)}, bf16[320,320]{0,1:T(8,128)(2,1)}, u32[]{:S(2)}, u32[]{:S(2)}) collective-permute-start(bf16[320,320]{0,1:T(8,128)(2,1)} %copy.9), channel_id=1, source_target_pairs={{288,0},{320,32},{352,64},{384,96},{416,128},{448,160},{480,192},{... | collective-permute-start | bytes 614408 | tf_op jit(solution)/shard_map/ppermute | solution.py:12
  476.5 0.2 copy.15
  476.7 0.2 copy.13
  476.9 0.2 copy.12
  477.1 0.2 copy.11
  477.3 0.2 copy.10
  477.5 7.0 collective-permute-start.1
  484.5 1.9 collective-permute-start.2
  486.4 1.9 collective-permute-start.3
  488.4 0.0 collective-permute-done.5
  488.4 4.5 collective-permute-start.4
  492.9 0.0 collective-permute-done
  492.9 1.9 collective-permute-start.6
  494.8 3.4 collective-permute-done.1
  498.2 0.0 collective-permute-done.2
  498.2 0.0 copy-start.2
  498.2 16.7 %collective-permute-done.3 = bf16[320,320]{0,1:T(8,128)(2,1)S(1)} collective-permute-done((bf16[320,320]{0,1:T(8,128)(2,1)S(1)}, bf16[320,320]{0,1:T(8,128)(2,1)S(1)}, u32[]{:S(2)}, u32[]{:S(2)}) %collective-permute-start.3) | collective-permute-done | bytes 204832 | tf_op jit(solution)/shard_map/ppermute | solution.py:12
  514.9 0.0 copy-start.3
  514.9 0.0 collective-permute-done.4
  514.9 0.0 copy-start.4
  514.9 0.0 collective-permute-done.6
  514.9 0.0 copy-done.2
  515.0 0.0 copy-start.5
  515.0 0.7 copy-done.3
  515.6 0.1 copy-done.4
  515.7 0.1 copy-done.5
  515.8 5.6 concatenate.6
  521.4 0.0 copy-start
  521.4 7.8 %convolution_convert_fusion = bf16[320,768]{1,0:T(8,128)(2,1)} fusion(bf16[320,5120]{1,0:T(8,128)(2,1)} %concatenate.6, bf16[5120,768]{1,0:T(8,128)(2,1)} %fusion.1), kind=kOutput, calls=%fused_computation.13 | convolution fusion | flops 2516828160 | bytes 11632640 | tf_op jit(solution)/shard_map/dot_general | solution.py:33
  529.2 0.0 all-gather.5.cloned.1.call-update
  529.3 182.0 %all-gather.5.cloned.1.call-done = bf16[5120,768]{1,0:T(8,128)(2,1)} async-done(((bf16[320,768]{1,0:T(8,128)(2,1)}), bf16[5120,768]{1,0:T(8,128)(2,1)}) %all-gather.5.cloned.1.call-update) | async-done | bytes 7864336 | tf_op jit(solution)/shard_map/all_gather | solution.py:34
  711.3 0.0 copy-done
  711.3 11.0 %fusion.15 = f32[320,768]{1,0:T(8,128)} fusion(bf16[320,5120]{1,0:T(8,128)(2,1)S(1)} %copy-done, s32[]{:T(128)S(6)} %select_n.13, bf16[5120,768]{1,0:T(8,128)(2,1)} %all-gather.5.cloned.1.call-done, bf16[320,768]{1,0:T(8,128)(2,1)} %convolution_convert_fusion, bf16[320,768]{1,0:T(8,128)(2,1)} %param.3), kind=kOutput, calls=%fused_computation.12 | convolution fusion | flops 2534277120 | bytes 13107204 | tf_op jit(solution)/shard_map/dot_general | solution.py:36
Async XLA Ops:
  6.5 188.2 %all-gather.3.cloned.1.call-start = ((), (), s32[]{:S(2)}) async-start(), calls=%async_computation | async-start | bytes 8355840 | tf_op jit(solution)/shard_map/all_gather | solution.py:20
  7.3 704.1 %all-gather.5.cloned.1.call-start = ((), (), s32[]{:S(2)}) async-start(), calls=%async_computation.1 | async-start | bytes 8355840 | tf_op jit(solution)/shard_map/all_gather | solution.py:34
  7.3 201.4 %copy-start.1 = (bf16[320,768]{1,0:T(8,128)(2,1)S(1)}, bf16[320,768]{1,0:T(8,128)(2,1)}, u32[]{:S(2)}) copy-start(bf16[320,768]{1,0:T(8,128)(2,1)} %param.3) | copy-start | bytes 1474564
  450.0 38.4 %collective-permute-start.5 = (bf16[320,320]{0,1:T(8,128)(2,1)}, bf16[320,320]{0,1:T(8,128)(2,1)}, u32[]{:S(2)}, u32[]{:S(2)}) collective-permute-start(bf16[320,320]{0,1:T(8,128)(2,1)} %copy.14), channel_id=1, source_target_pairs={{448,0},{480,32},{0,64},{32,96},{64,128},{96,160},{128,192},{160,2... | collective-permute-start | bytes 614408 | tf_op jit(solution)/shard_map/ppermute | solution.py:12
  452.8 40.1 %collective-permute-start = (bf16[320,320]{0,1:T(8,128)(2,1)}, bf16[320,320]{0,1:T(8,128)(2,1)}, u32[]{:S(2)}, u32[]{:S(2)}) collective-permute-start(bf16[320,320]{0,1:T(8,128)(2,1)} %copy.9), channel_id=1, source_target_pairs={{288,0},{320,32},{352,64},{384,96},{416,128},{448,160},{480,192},{... | collective-permute-start | bytes 614408 | tf_op jit(solution)/shard_map/ppermute | solution.py:12
  477.5 20.7 %collective-permute-start.1 = (bf16[320,320]{0,1:T(8,128)(2,1)S(1)}, bf16[320,320]{0,1:T(8,128)(2,1)S(1)}, u32[]{:S(2)}, u32[]{:S(2)}) collective-permute-start(bf16[320,320]{0,1:T(8,128)(2,1)S(1)} %copy.10), channel_id=1, source_target_pairs={{320,0},{352,32},{384,64},{416,96},{448,128},{480,160},{0,192},{32... | collective-permute-start | bytes 614408 | tf_op jit(solution)/shard_map/ppermute | solution.py:12
  484.5 13.7 %collective-permute-start.2 = (bf16[320,320]{0,1:T(8,128)(2,1)S(1)}, bf16[320,320]{0,1:T(8,128)(2,1)S(1)}, u32[]{:S(2)}, u32[]{:S(2)}) collective-permute-start(bf16[320,320]{0,1:T(8,128)(2,1)S(1)} %copy.11), channel_id=1, source_target_pairs={{352,0},{384,32},{416,64},{448,96},{480,128},{0,160},{32,192},{64,... | collective-permute-start | bytes 614408 | tf_op jit(solution)/shard_map/ppermute | solution.py:12
  486.4 28.5 %collective-permute-start.3 = (bf16[320,320]{0,1:T(8,128)(2,1)S(1)}, bf16[320,320]{0,1:T(8,128)(2,1)S(1)}, u32[]{:S(2)}, u32[]{:S(2)}) collective-permute-start(bf16[320,320]{0,1:T(8,128)(2,1)S(1)} %copy.12), channel_id=1, source_target_pairs={{384,0},{416,32},{448,64},{480,96},{0,128},{32,160},{64,192},{96,2... | collective-permute-start | bytes 614408 | tf_op jit(solution)/shard_map/ppermute | solution.py:12
  488.4 26.6 %collective-permute-start.4 = (bf16[320,320]{0,1:T(8,128)(2,1)S(1)}, bf16[320,320]{0,1:T(8,128)(2,1)S(1)}, u32[]{:S(2)}, u32[]{:S(2)}) collective-permute-start(bf16[320,320]{0,1:T(8,128)(2,1)S(1)} %copy.13), channel_id=1, source_target_pairs={{416,0},{448,32},{480,64},{0,96},{32,128},{64,160},{96,192},{128,2... | collective-permute-start | bytes 614408 | tf_op jit(solution)/shard_map/ppermute | solution.py:12
  492.9 22.0 %collective-permute-start.6 = (bf16[320,320]{0,1:T(8,128)(2,1)S(1)}, bf16[320,320]{0,1:T(8,128)(2,1)S(1)}, u32[]{:S(2)}, u32[]{:S(2)}) collective-permute-start(bf16[320,320]{0,1:T(8,128)(2,1)S(1)} %copy.15), channel_id=1, source_target_pairs={{480,0},{0,32},{32,64},{64,96},{96,128},{128,160},{160,192},{192,2... | collective-permute-start | bytes 614408 | tf_op jit(solution)/shard_map/ppermute | solution.py:12
  498.2 16.7 %copy-start.2 = (bf16[320,320]{0,1:T(8,128)(2,1)}, bf16[320,320]{0,1:T(8,128)(2,1)S(1)}, u32[]{:S(2)}) copy-start(bf16[320,320]{0,1:T(8,128)(2,1)S(1)} %collective-permute-done.2) | copy-start | bytes 614404
  514.9 0.7 copy-start.3
  514.9 0.8 copy-start.4
  515.0 0.8 copy-start.5
  521.4 189.9 %copy-start = (bf16[320,5120]{1,0:T(8,128)(2,1)S(1)}, bf16[320,5120]{1,0:T(8,128)(2,1)}, u32[]{:S(2)}) copy-start(bf16[320,5120]{1,0:T(8,128)(2,1)} %concatenate.6) | copy-start | bytes 9830404
Sparse Core Ops, SparseCore 0:
  9.4 185.2 all-gather.2
  529.4 181.8 all-gather.4
where the time goes:
time: 730 us; the launch traced here: 729 us
  waiting for transfers between devices  390 us (53%)
  blocking collectives  232 us (32%)
  starting transfers between devices  43 us (6%)
  matrix products  24.7 us (3%)
  other arithmetic  13.9 us (2%)
  between operations  13.6 us (2%)
  local copies, waits for them, and re-layouts  11.2 us (2%)
    psum x1, blocking collectives, local(): gram = lax.psum(band, 'col').astype(jnp.bfloat16)  232 us
    all_gather x1, waiting for transfers between devices, local(): gathered = lax.all_gather(iterate, 'row', axis=0, tiled=True)  187 us
    all_gather x1, waiting for transfers between devices, local(): image_all = lax.all_gather(image, 'row', axis=0, tiled=True)  182 us
    ppermute x7, starting transfers between devices, shifted(): return lax.ppermute(block, axis, route)  42.9 us
    ppermute x7, waiting for transfers between devices, shifted(): return lax.ppermute(block, axis, route)  20.1 us
  transfers between devices with their start and end apart: 9, of which 4 were waited for; matrix products, arithmetic and copies ran while one was open for 0% of the time, Pallas kernels for 0%

commit v1 on v0

v1 whole, which is shorter than its diff:
```python
import functools

import jax
import jax.numpy as jnp
from jax import lax
from jax.experimental import pallas as pl
from jax.experimental.pallas import tpu as pltpu
from jax.sharding import PartitionSpec as P

HID = 24576
FACTOR = 0.2 * HID**0.5
MESH = pl.DeviceIdType.MESH
F32 = jnp.float32
BF16 = jnp.bfloat16
NT = (((1,), (1,)), ((), ()))


def pick(index, *values):
    out = values[-1]
    for i in range(len(values) - 2, -1, -1):
        out = jnp.where(index == i, values[i], out)
    return out


def ring(i, distance):
    return lax.rem(i + distance + 4, 4)


def visit(i):
    m = lax.rem(i, 4)
    code = jnp.where(i < 4, jnp.maximum(i - 1, 0), jnp.where(i < 12, m, jnp.where(i < 14, i - 11, 3)))
    middle = lax.div(i, 4) + (m == 0).astype(jnp.int32) - (m == 3).astype(jnp.int32)
    rank = jnp.where(i < 4, (i == 1).astype(jnp.int32), jnp.where(i < 12, middle, jnp.where(i < 14, 3, i - 12)))
    return code, rank


def chain_order(z, t):
    low = jnp.minimum(z, 3 - z)
    base = jnp.where((low == 1) & (t < 2), 1 - t, t)
    return jnp.where(z < 2, base, 3 - base)


def tile_of(zh, y):
    return zh * 4 + ring(y, -zh)


def kernel(
    x_ref, out_ref, xg, own, csend, crecv, ysend, yrecv, zsend, zrecv, gl, gr, ng,
    xs_sem, xr_sem, cs_sem, cr_sem, ys_sem, yr_sem, zs_sem, zr_sem,
    ls_sem, lr_sem, rs_sem, rr_sem, hs_sem, hr_sem, ns_sem, nr_sem, ms_sem, mr_sem,
):
    rows = x_ref.shape[0]
    half = rows // 2
    me = lax.axis_index("row")
    place = lax.axis_index("col")
    x, z = lax.div(me, 4), lax.rem(me, 4)
    zh, y, core = lax.div(place, 8), lax.rem(lax.div(place, 2), 4), lax.rem(place, 2)
    mine = tile_of(zh, y)

    def col_at(a, b):
        return {"col": (a * 4 + b) * 2 + core}

    partner = {"col": (zh * 4 + y) * 2 + 1 - core}

    barrier = pltpu.get_barrier_semaphore()

    def greet(device):
        pl.semaphore_signal(barrier, inc=1, device_id=device, device_id_type=MESH)

    greet({"row": ring(x, 1) * 4 + z})
    greet({"row": ring(x, -1) * 4 + z})
    pl.when(z < 3)(lambda: greet({"row": me + 1}))
    pl.when(z > 0)(lambda: greet({"row": me - 1}))
    greet(partner)
    for d in range(1, 4):
        greet(col_at(zh, ring(y, d)))
        greet(col_at(ring(zh, d), y))
    peers = 9 + (z < 3).astype(jnp.int32) + (z > 0).astype(jnp.int32)
    xg[me] = x_ref[...]
    pl.semaphore_wait(barrier, peers)

    def remote(src, dst, ssem, rsem, device):
        return pltpu.make_async_remote_copy(
            src_ref=src, dst_ref=dst, send_sem=ssem, recv_sem=rsem, device_id=device, device_id_type=MESH
        )

    def row_slot(i):
        code, t = visit(i)
        return pick(code, x, ring(x, -1), ring(x, 1), ring(x, 2)) * 4 + chain_order(z, t)

    def row_ops(full, part, ssem, rsem):
        def send(ref, sem, rcv, target):
            return remote(ref, ref, ssem.at[sem], rcv, {"row": target})

        right, left = ring(x, 1) * 4 + z, ring(x, -1) * 4 + z

        def to_right(slot, b):
            return send(full(slot), 8 + b, rsem.at[slot, 0], right)

        def to_left(slot, b):
            return send(full(slot), 12 + b, rsem.at[slot, 0], left)

        def on_right(slot, b):
            return send(part(slot, 0), 16 + b, rsem.at[slot, 0], right)

        def on_left(slot, b):
            return send(part(slot, 1), 20 + b, rsem.at[slot, 1], left)

        def up(slot, b):
            return send(full(slot), b, rsem.at[slot, 0], me + 1)

        def down(slot, b):
            return send(full(slot), 4 + b, rsem.at[slot, 0], me - 1)

        def step(i):
            code, t = visit(i)
            b = chain_order(z, t)
            slot = row_slot(i)

            @pl.when(((code == 0) & (t > 0)) | (code == 1) | (code == 2))
            def _():
                to_right(slot, b).wait_recv()

            @pl.when(code == 0)
            def _():
                pl.when((b <= z) & (z < 3))(lambda: up(slot, b).start())
                pl.when((b >= z) & (z > 0))(lambda: down(slot, b).start())
                to_right(slot, b).start()
                to_left(slot, b).start()

            pl.when(code == 1)(lambda: on_right(slot, b).start())
            pl.when(code == 2)(lambda: on_left(slot, b).start())

            @pl.when(code == 3)
            def _():
                on_right(slot, b).wait_recv()
                on_left(slot, b).wait_recv()

        def drain():
            def body(b, _):
                slot = x * 4 + b
                pl.when((b <= z) & (z < 3))(lambda: up(slot, b).wait_send())
                pl.when((b >= z) & (z > 0))(lambda: down(slot, b).wait_send())
                to_right(slot, b).wait_send()
                to_left(slot, b).wait_send()
                on_right(slot, b).wait_send()
                on_left(slot, b).wait_send()
                return 0

            lax.fori_loop(0, 4, body, 0)

        return step, drain

    def col_tile(i):
        code, t = visit(i)
        a = pick(t, zh, ring(zh, -1), ring(zh, 1), ring(zh, 2))
        b = pick(code, y, ring(y, -1), ring(y, 1), ring(y, 2))
        return tile_of(a, b)

    def col_ops(full, part, ssem, rsem):
        def send(ref, sem, rcv, target):
            return remote(ref, ref, ssem.at[sem], rcv, target)

        up, down = col_at(ring(zh, 1), y), col_at(ring(zh, -1), y)
        right, left = col_at(zh, ring(y, 1)), col_at(zh, ring(y, -1))

        def z_up(k):
            return send(full(k), 0, rsem.at[k, 0], up)

        def z_down(k):
            return send(full(k), 1, rsem.at[k, 0], down)

        def z_on_up(k):
            return send(part(k, 0), 2, rsem.at[k, 0], up)

        def z_on_down(k):
            return send(part(k, 1), 3, rsem.at[k, 1], down)

        def to_right(k, t):
            return send(full(k), 4 + t, rsem.at[k, 0], right)

        def to_left(k, t):
            return send(full(k), 8 + t, rsem.at[k, 0], left)

        def on_right(k, t):
            return send(part(k, 0), 12 + t, rsem.at[k, 0], right)

        def on_left(k, t):
            return send(part(k, 1), 16 + t, rsem.at[k, 1], left)

        def step(i):
            code, t = visit(i)
            k = col_tile(i)

            @pl.when(((code == 0) & ((t == 1) | (t == 2))) | (code == 1) | (code == 2))
            def _():
                to_right(k, t).wait_recv()

            @pl.when((code == 3) | ((code == 0) & (t == 3)))
            def _():
                on_right(k, t).wait_recv()
                on_left(k, t).wait_recv()

            @pl.when(code == 0)
            def _():
                @pl.when(t == 0)
                def _():
                    z_up(k).start()
                    z_down(k).start()

                pl.when(t == 1)(lambda: z_on_up(k).start())
                pl.when(t == 2)(lambda: z_on_down(k).start())
                to_right(k, t).start()
                to_left(k, t).start()

            pl.when(code == 1)(lambda: on_right(k, t).start())
            pl.when(code == 2)(lambda: on_left(k, t).start())

        def drain():
            for copy in (z_up(mine), z_down(mine), z_on_up(mine), z_on_down(mine)):
                copy.wait_send()

            def body(t, _):
                for copy in (to_right, to_left, on_right, on_left):
                    copy(mine, t).wait_send()
                return 0

            lax.fori_loop(0, 4, body, 0)

        return step, drain

    low = pl.multiple_of(core * half, 32)
    high = pl.multiple_of((1 - core) * half, 32)

    x_step, x_drain = row_ops(
        lambda s: xg.at[s], lambda s, w: xg.at[s, pl.ds(w * half, half)], xs_sem, xr_sem
    )

    def across(k):
        return remote(csend.at[k], crecv.at[k], cs_sem.at[k], cr_sem.at[k], partner)

    def y_send(k, d):
        return remote(
            ysend.at[k], yrecv.at[lax.div(k, 4), d - 1], ys_sem.at[k], yr_sem.at[lax.div(k, 4), d - 1],
            col_at(zh, ring(y, d)),
        )

    def core_sum(k):
        across(k).wait_recv()
        total = own[k] + crecv[k].astype(F32)
        d = ring(lax.div(k, 4) + lax.rem(k, 4), -y)

        @pl.when(lax.rem(d, 4) == 0)
        def _():
            own[k] = total

        @pl.when(lax.rem(d, 4) != 0)
        def _():
            ysend[k] = total.astype(BF16)
            y_send(k, lax.rem(d, 4)).start()

    def z_send(a, d):
        return remote(zsend.at[a], zrecv.at[d - 1], zs_sem.at[a], zr_sem.at[d - 1], col_at(ring(zh, d), y))

    def y_sum(a):
        k = tile_of(a, y)
        total = own[k]
        for d in range(1, 4):
            y_send(a * 4, d).wait_recv()
            total = total + yrecv[a, d - 1].astype(F32)
        d = ring(a, -zh)

        @pl.when(d == 0)
        def _():
            own[k] = total

        @pl.when(d != 0)
        def _():
            zsend[a] = total.astype(BF16)
            z_send(a, d).start()

    def x_body(i, _):
        pl.when(i == 14)(lambda: y_sum(x))

        @pl.when(i == 15)
        def _():
            y_sum(ring(x, -1))
            y_sum(ring(x, 1))

        x_step(i)
        k = row_slot(i)
        csend[k] = lax.dot_general(x_ref[pl.ds(high, half)], xg[k], NT, preferred_element_type=F32).astype(BF16)
        across(k).start()
        own[k] = lax.dot_general(x_ref[pl.ds(low, half)], xg[k], NT, preferred_element_type=F32)
        pl.when(i > 0)(lambda: core_sum(row_slot(i - 1)))
        return 0

    lax.fori_loop(0, 16, x_body, 0)
    core_sum(row_slot(jnp.int32(15)))
    y_sum(ring(x, 2))
    total = own[mine]
    for d in range(1, 4):
        z_send(zh, d).wait_recv()
        total = total + zrecv[d - 1].astype(F32)
    gl[mine] = total.astype(BF16)
    gr[me, pl.ds(low, half)] = total.astype(BF16)

    quarter = half // 2
    l_step, l_drain = col_ops(
        lambda k: gl.at[k], lambda k, w: gl.at[k, pl.ds(w * quarter, quarter)], ls_sem, lr_sem
    )
    r_step, r_drain = row_ops(
        lambda s: gr.at[s, pl.ds(low, half)],
        lambda s, w: gr.at[s, pl.ds(pl.multiple_of(core * half + w * quarter, 16), quarter)],
        rs_sem, rr_sem,
    )

    def halves(ref, s, ssem, rsem):
        return remote(ref.at[s, pl.ds(low, half)], ref.at[s, pl.ds(low, half)], ssem.at[s], rsem.at[s], partner)

    def g_body(i, _):
        l_step(i)
        r_step(i)
        halves(gr, row_slot(i), hs_sem, hr_sem).start()
        return 0

    lax.fori_loop(0, 16, g_body, 0)

    def n_body(k, total):
        halves(gr, k, hs_sem, hr_sem).wait_recv()
        return total + jnp.dot(gl[k], gr[k], preferred_element_type=F32)

    square = lax.fori_loop(0, 16, n_body, jnp.zeros((half, rows), F32))
    ng[mine, pl.ds(low, half)] = (4.775 * gl[mine].astype(F32) - 2.0315 * square).astype(BF16)

    n_step, n_drain = col_ops(
        lambda k: ng.at[k, pl.ds(low, half)],
        lambda k, w: ng.at[k, pl.ds(pl.multiple_of(core * half + w * quarter, 16), quarter)],
        ns_sem, nr_sem,
    )
    out_ref[...] = (FACTOR * 3.4445) * x_ref[...].astype(F32)

    def product(k):
        halves(ng, k, ms_sem, mr_sem).wait_recv()
        out_ref[...] -= FACTOR * jnp.dot(ng[k], xg[k], preferred_element_type=F32)

    def o_body(i, _):
        n_step(i)
        halves(ng, col_tile(i), ms_sem, mr_sem).start()
        pl.when(i > 0)(lambda: product(col_tile(i - 1)))
        return 0

    lax.fori_loop(0, 16, o_body, 0)
    product(col_tile(jnp.int32(15)))

    x_drain()
    l_drain()
    r_drain()
    n_drain()

    def end(k, _):
        across(k).wait_send()
        halves(gr, k, hs_sem, hr_sem).wait_send()
        halves(ng, k, ms_sem, mr_sem).wait_send()
        d = ring(lax.div(k, 4) + lax.rem(k, 4), -y)
        pl.when(lax.rem(d, 4) != 0)(lambda: y_send(k, 1).wait_send())
        return 0

    lax.fori_loop(0, 16, end, 0)

    def z_end(a, _):
        pl.when(a != zh)(lambda: z_send(a, 1).wait_send())
        return 0

    lax.fori_loop(0, 4, z_end, 0)


def local(iterate):
    rows, columns = iterate.shape
    half = rows // 2
    dma = pltpu.SemaphoreType.DMA
    vmem = pltpu.VMEM
    return pl.pallas_call(
        kernel,
        out_shape=jax.ShapeDtypeStruct((rows, columns), F32),
        in_specs=[pl.BlockSpec(memory_space=pltpu.VMEM)],
        out_specs=pl.BlockSpec(memory_space=pltpu.VMEM),
        scratch_shapes=[
            vmem((16, rows, columns), BF16),
            vmem((16, half, rows), F32),
            vmem((16, half, rows), BF16),
            vmem((16, half, rows), BF16),
            vmem((16, half, rows), BF16),
            vmem((4, 3, half, rows), BF16),
            vmem((4, half, rows), BF16),
            vmem((3, half, rows), BF16),
            vmem((16, half, rows), BF16),
            vmem((16, rows, rows), BF16),
            vmem((16, rows, rows), BF16),
            dma((24,)), dma((16, 2)),
            dma((16,)), dma((16,)),
            dma((16,)), dma((4, 3)),
            dma((4,)), dma((3,)),
            dma((20,)), dma((16, 2)),
            dma((24,)), dma((16, 2)),
            dma((16,)), dma((16,)),
            dma((20,)), dma((16, 2)),
            dma((16,)), dma((16,)),
        ],
        compiler_params=pltpu.CompilerParams(
            collective_id=0, has_side_effects=True, vmem_limit_bytes=48 * 2**20
        ),
        name="newton_schulz",
    )(iterate)


def solution(mesh):
    in_specs = (P("row", "col"),)
    out_specs = P("row", "col")
    return jax.shard_map(local, mesh=mesh, in_specs=in_specs, out_specs=out_specs, check_vma=False)
```

time: 730 us -> 189 us (0.26)
  waiting for transfers between devices: 390 us -> 0 us
  blocking collectives: 232 us -> 0 us
  Pallas kernels: 0 us -> 187 us
  starting transfers between devices: 43 us -> 0 us
  matrix products: 24.7 us -> 0 us
  other arithmetic: 13.9 us -> 0 us
  between operations: 13.6 us -> 0.01 us
  local copies, waits for them, and re-layouts: 11.2 us -> 1.98 us
    all_gather x2 -> x0, waiting for transfers between devices: 369 us -> none  [the longest x1 187 us: local(): gathered = lax.all_gather(iterate, 'row', axis=0, tiled=True)]
    psum x1 -> x0, blocking collectives: 232 us -> none  [local(): gram = lax.psum(band, 'col').astype(jnp.bfloat16)]
    pallas_call x0 -> x1, Pallas kernels: none -> 187 us  [local(): pl.pallas_call(kernel, out_shape=jax.ShapeDtypeStruct((rows, columns), F3...]
    ppermute x7 -> x0, starting transfers between devices: 42.9 us -> none  [shifted(): return lax.ppermute(block, axis, route)]
    dot_general x3 -> x0, matrix products: 24.7 us -> none  [the longest x1 11 us: local(): jnp.dot(row_block, image_rolled, preferred_element_type=jnp.float32)]
    ppermute x7 -> x0, waiting for transfers between devices: 20.1 us -> none  [shifted(): return lax.ppermute(block, axis, route)]
    concatenate x1 -> x0, other arithmetic: 13.9 us -> none  [local(): rolled = jnp.roll(gathered, -mine * rows, axis=0)]
  transfers between devices with their start and end apart: 9 -> 0, of which waited for: 4 -> 0; matrix products, arithmetic and copies ran while one was open for 0% -> 0% of each run, Pallas kernels for 0% -> 0%
where the time goes in v1:
time: 189 us
  Pallas kernels  187 us (99%)
  local copies, waits for them, and re-layouts  1.98 us (1%)
    pallas_call x1, Pallas kernels, local(): pl.pallas_call(kernel, out_shape=jax.ShapeDtypeStruct((rows, columns), F3...  187 us

profile of v1, /device:TPU:1, one launch (start us, length us, event | category | flops | bytes accessed | tf_op | source)
XLA Modules:
  0.0 189.0 jit_solution(14775161298004750914)
XLA Ops:
  0.0 0.0 copy-start
  0.0 1.0 copy-done
  1.0 187.0 %newton_schulz.1 = f32[320,768]{1,0:T(8,128)S(1)} custom-call(bf16[320,768]{1,0:T(8,128)(2,1)S(1)} %copy-done), custom_call_target="tpu_custom_call" | custom-call | tf_op jit(solution)/shard_map/newton_schulz/pallas_call | solution.py:383
  188.1 0.9 copy.3
Async XLA Ops:
  0.0 1.0 copy-start
